TPU v7x, 32 devices: a whole 2x2x4 slice. The times are simulated.
32 devices in a mesh: lat: 8 (over y, x, core), chan: 4 (over z).
Axes of the slice: x: 2, y: 2, z: 4, core: 2. Of those that a mesh axis runs over, the one named last changes fastest.
Arguments:
- grid_field: bfloat16 [8, 2, 384, 1440], P('lat', None, 'chan'), may hold values from -6 to 6
- cotangent: bfloat16 [8, 2, 384, 1440], P('lat', None, 'chan'), may hold values from -6 to 6
- legendre: bfloat16 [40, 1361, 8], P('lat'), may hold values from -1.5 to 1.5
- spectral: float32 [384, 2, 720], P('chan'), may hold values from -3 to 3
- mixing: bfloat16 [384, 384], P(None, 'chan'), may hold values from -0.3125 to 0.3125
- pair_table: int32 [40], replicated, may hold values from 0 to 39, each once
Outputs:
- block_output: bfloat16 [8, 2, 384, 1440], P('lat', None, 'chan')
- grad_input: bfloat16 [8, 2, 384, 1440], P('lat', None, 'chan')
- grad_weights: float32 [384, 2, 720], P('chan')
- grad_mixing: float32 [384, 384], P(None, 'chan')
Inputs may be any that keep to these rules, and one draw needn't show every extreme that they name: `pair_table`: each pair p stands for the orders p and 79 - p, whose degree ranges together fill 1361 coefficients. Index i of lat owns the slots i * 5 to (i + 1) * 5 - 1.
All inputs are finite; a program needn't handle non-finite values.
Results may differ from a plain program's by a relative error of at most 0.0067.
Values may be sent and summed in bfloat16 or wider, within the bound.
A program may use at most 128 MiB of HBM per device.

v0:
```python
import math
import jax
import jax.numpy as jnp
from jax import lax
from jax.sharding import PartitionSpec as P


def dft_basis(orders, longitudes):
    lon_index = jnp.arange(longitudes, dtype=jnp.int32)
    turns = lon_index[:, None] * orders[None, :] % longitudes
    angles = turns.astype(jnp.float32) * (2.0 * math.pi / longitudes)
    norm_scale = 1.0 / math.sqrt(longitudes)
    basis = jnp.stack([jnp.cos(angles) * norm_scale, -jnp.sin(angles) * norm_scale], axis=1)
    return basis.astype(jnp.bfloat16)


def even_odd(spectrum):
    return jnp.stack(
        [spectrum[:, 0] + spectrum[:, 1], spectrum[:, 0] - spectrum[:, 1]], axis=1
    ).astype(jnp.bfloat16)


def local(grid_field, cotangent, legendre, spectral, mixing, pair_table):
    lat_count = lax.axis_size("lat")
    owned = legendre.shape[0]
    packed = legendre.shape[1]
    npairs = legendre.shape[2]
    degrees = spectral.shape[2]
    chan_width = grid_field.shape[2]
    longitudes = grid_field.shape[3]
    order_count = 2 * owned * lat_count
    slot_orders = jnp.stack([pair_table, order_count - 1 - pair_table], axis=1).reshape(-1)
    basis = dft_basis(slot_orders, longitudes)
    weight_m = jnp.where(slot_orders == 0, 1.0, 2.0).astype(jnp.float32)
    spec_x = jnp.einsum("khcj,jrm->khcrm", grid_field, basis, preferred_element_type=jnp.float32)
    spec_g = (
        jnp.einsum("khcj,jrm->khcrm", cotangent, basis, preferred_element_type=jnp.float32)
        * weight_m
    )
    recv_x, recv_g = (
        lax.all_to_all(even_odd(spec_x), "lat", split_axis=4, concat_axis=0, tiled=True),
        lax.all_to_all(even_odd(spec_g), "lat", split_axis=4, concat_axis=0, tiled=True),
    )
    owner_shape = (npairs, 2, chan_width, 2, owned, 2)
    recv_x = recv_x.reshape(owner_shape)
    recv_g = recv_g.reshape(owner_shape)
    slot_start = lax.axis_index("lat") * owned
    lower = lax.dynamic_slice_in_dim(pair_table, slot_start, owned)
    position = jnp.arange(packed, dtype=jnp.int32)[None, :]
    lower_col = lower[:, None]
    leading = position < degrees - lower_col
    degree = jnp.where(leading, lower_col + position, position - (degrees - order_count + 1))
    order = jnp.where(leading, lower_col, order_count - 1 - lower_col)
    half_pick = jnp.where(leading, 0, 1)
    parity = (degree + order) % 2
    two_index = jnp.arange(2, dtype=jnp.int32)
    selector = (
        (half_pick[:, None, None, :] == two_index[None, :, None, None])
        & (parity[:, None, None, :] == two_index[None, None, :, None])
    ).astype(jnp.float32)

    def analyse(received):
        variants = jnp.einsum(
            "pqk,kecrph->phercq", legendre, received, preferred_element_type=jnp.float32
        )
        return jnp.sum(variants * selector[:, :, :, None, None, :], axis=(1, 2))

    coeff_x = analyse(recv_x)
    coeff_g = analyse(recv_g)
    weight_rows = jnp.transpose(spectral, (1, 0, 2))
    weight_pad = jnp.concatenate(
        [weight_rows, jnp.zeros((2, chan_width, packed), jnp.float32)], axis=2
    )
    weight_tail = jnp.concatenate(
        [jnp.zeros((2, chan_width, degrees - order_count + 1), jnp.float32), weight_rows], axis=2
    )
    picked_lead = jnp.stack(
        [lax.dynamic_slice_in_dim(weight_pad, lower[slot], packed, 2) for slot in range(owned)]
    )
    picked = jnp.where(leading[:, None, None, :], picked_lead, weight_tail[None])
    real_w, imag_w = (picked[:, 0], picked[:, 1])
    real_x, imag_x = (coeff_x[:, 0], coeff_x[:, 1])
    real_g, imag_g = (coeff_g[:, 0], coeff_g[:, 1])
    filtered = jnp.stack(
        [real_w * real_x - imag_w * imag_x, real_w * imag_x + imag_w * real_x], axis=1
    ).astype(jnp.bfloat16)
    back_coeff = jnp.stack(
        [real_w * real_g + imag_w * imag_g, real_w * imag_g - imag_w * real_g], axis=1
    ).astype(jnp.bfloat16)
    grad_term = jnp.stack(
        [real_g * real_x + imag_g * imag_x, imag_g * real_x - real_g * imag_x], axis=1
    )
    grad_rows = jnp.zeros((2, chan_width, degrees + packed), jnp.float32)
    for slot in range(owned):
        head_part = jnp.where(leading[slot][None, None, :], grad_term[slot], 0.0)
        current = lax.dynamic_slice_in_dim(grad_rows, lower[slot], packed, 2)
        grad_rows = lax.dynamic_update_slice_in_dim(grad_rows, current + head_part, lower[slot], 2)
    tail_part = jnp.sum(jnp.where(leading[:, None, None, :], 0.0, grad_term), axis=0)
    grad_local = jnp.transpose(
        grad_rows[:, :, :degrees] + tail_part[:, :, degrees - order_count + 1 :], (1, 0, 2)
    )

    def synthesize(coeff):
        masked = (
            coeff[:, None, None].astype(jnp.float32) * selector[:, :, :, None, None, :]
        ).astype(jnp.bfloat16)
        both = jnp.einsum(
            "pqk,phercq->kecrph", legendre, masked, preferred_element_type=jnp.float32
        )
        return even_odd(both.reshape(npairs, 2, chan_width, 2, 2 * owned))

    row_y, row_dx = (
        lax.all_to_all(synthesize(filtered), "lat", split_axis=0, concat_axis=4, tiled=True),
        lax.all_to_all(synthesize(back_coeff), "lat", split_axis=0, concat_axis=4, tiled=True),
    )
    filtered_grid = jnp.einsum(
        "khcrm,jrm->khcj",
        row_y * weight_m.astype(jnp.bfloat16),
        basis,
        preferred_element_type=jnp.float32,
    )
    back_grid = jnp.einsum("khcrm,jrm->khcj", row_dx, basis, preferred_element_type=jnp.float32)
    field_full, cot_full, mixing_full = (
        lax.all_gather(grid_field, "chan", axis=2, tiled=True),
        lax.all_gather(cotangent, "chan", axis=2, tiled=True),
        lax.all_gather(mixing, "chan", axis=1, tiled=True),
    )
    mixing_own = lax.dynamic_slice_in_dim(
        mixing_full, lax.axis_index("chan") * chan_width, chan_width, 0
    )
    skip_path = jnp.einsum("khij,io->khoj", field_full, mixing, preferred_element_type=jnp.float32)
    back_skip = jnp.einsum(
        "khoj,io->khij", cot_full, mixing_own, preferred_element_type=jnp.float32
    )
    mixing_grad = jnp.einsum(
        "khij,khoj->io", field_full, cotangent, preferred_element_type=jnp.float32
    )
    block_output = (filtered_grid + skip_path).astype(jnp.bfloat16)
    grad_input = (back_grid + back_skip).astype(jnp.bfloat16)
    weight_sum, mixing_sum = lax.psum((grad_local, mixing_grad), "lat")
    grad_weights = weight_sum / math.sqrt(order_count)
    grad_mixing = mixing_sum / math.sqrt(2 * npairs * longitudes)
    return (block_output, grad_input, grad_weights, grad_mixing)


def solution(mesh):
    in_specs = (
        P("lat", None, "chan", None),
        P("lat", None, "chan", None),
        P("lat", None, None),
        P("chan", None, None),
        P(None, "chan"),
        P(),
    )
    out_specs = (
        P("lat", None, "chan", None),
        P("lat", None, "chan", None),
        P("chan", None, None),
        P(None, "chan"),
    )
    return jax.shard_map(local, mesh=mesh, in_specs=in_specs, out_specs=out_specs, check_vma=False)
```

profile of v0, /device:TPU:0, one launch (start us, length us, event | category | flops | bytes accessed | tf_op | source)
XLA Modules:
  0.0 241.8 jit_solution(9440944002188104553)
XLA Ops:
  7.2 2.6 %copy.56 = bf16[1,2,96,1440]{3,1,0,2:T(2,128)(2,1)} copy(bf16[1,2,96,1440]{3,2,1,0:T(8,128)(2,1)} %param.6) | data formatting | bytes 1105920 | tf_op args[0]
  9.8 0.7 subtract_bitcast_fusion
  11.9 2.2 multiply_convert_fusion.3
  14.2 1.6 fusion.16
  16.6 5.2 %all-to-all-start.2 = ((bf16[1,2,96,2,80]{2,1,3,0,4:T(2,128)(2,1)}), bf16[1,2,96,2,80]{2,1,3,0,4:T(2,128)(2,1)S(1)}, u32[]{:S(2)}, u32[]{:S(2)}) async-start(bf16[1,2,96,2,80]{2,1,3,0,4:T(2,128)(2,1)} %copy.58), calls=%async_computation.2 | async-start | bytes 163840 | tf_op jit(solution)/shard_map/all_to_all | solution.py:42
  21.9 1.4 copy.68
  34.2 3.9 %pad_dynamic-slice_fusion = (f32[2,96,1361]{2,0,1:T(2,128)S(1)}, f32[2,96,1361]{2,0,1:T(2,128)S(1)}, f32[2,96,1361]{2,0,1:T(2,128)S(1)}, f32[2,96,1361]{2,0,1:T(2,128)S(1)}, f32[2,96,1361]{2,0,1:T(2,128)S(1)}) fusion(s32[]{:T(128)S(6)} %select_n.122, f32[2,96,720]{2,0,1:T(2,128)S(1)} %bitcast.169, s32[]{:T(128)S(6)} %select_n.119, s32[]{:T(128)S(6)} %select_n.120, ...), kind=kLoop, calls=%fused_computation.40 | loop fusion | bytes 5779220 | tf_op jit(solution)/shard_map/dynamic_slice | solution.py:78
  38.9 2.8 %broadcast_select_fusion = f32[5,2,96,1361]{3,2,1,0:T(8,128)} fusion(f32[5,2,96,1361]{3,2,1,0:T(8,128)S(1)} %bitcast_dynamic-update-slice_fusion, f32[2,96,1361]{2,1,0:T(8,128)S(1)} %concatenate.35.clone, pred[5,1361]{1,0:T(8,128)(4,1)S(1)} %iota_compare_fusion.2), kind=kLoop, calls=%fused_computation.31 | loop fusion | flops 1306560 | bytes 11504533 | tf_op jit(solution)/shard_map/jit(_where)/select_n | solution.py:80
  41.9 17.9 %all_gather.10 = bf16[384,384]{0,1:T(8,128)(2,1)} all-gather(bf16[384,96]{0,1:T(8,128)(2,1)S(1)} %copy-done.17), channel_id=1, replica_groups=mesh['lat'=8,'chan'=4] {'chan'}, dimensions={1}, use_global_device_ids=true | all-gather | bytes 368640 | tf_op jit(solution)/shard_map/all_gather | solution.py:126
  60.6 4.1 %all-to-all-start = ((bf16[1,2,96,2,80]{2,1,3,0,4:T(2,128)(2,1)}), bf16[1,2,96,2,80]{2,1,3,0,4:T(2,128)(2,1)S(1)}, u32[]{:S(2)}, u32[]{:S(2)}) async-start(bf16[1,2,96,2,80]{2,1,3,0,4:T(2,128)(2,1)} %copy.47), calls=%async_computation | async-start | bytes 163840 | tf_op jit(solution)/shard_map/all_to_all | solution.py:41
  64.7 6.0 %fusion = f32[5,2,96,1361]{3,2,1,0:T(8,128)} fusion(f32[5,2,2,1361]{3,1,2,0:T(2,128)S(1)} %and_convert_fusion, bf16[5,1361,8]{1,2,0:T(8,128)(2,1)S(1)} %copy-done, bf16[8,2,96,2,5,2]{2,1,3,5,4,0:T(2,128)(2,1)S(1)} %bitcast.176), kind=kOutput, calls=%fused_computation.1 | convolution fusion | flops 92765760 | bytes 5505440 | tf_op jit(solution)/shard_map/pqk,kecrph->phercq/dot_general | solution.py:63
  70.7 3.7 %fusion.1 = f32[5,2,96,1361]{3,2,1,0:T(8,128)S(1)} fusion(f32[5,2,2,1361]{3,1,2,0:T(2,128)S(1)} %and_convert_fusion, bf16[5,1361,8]{1,2,0:T(8,128)(2,1)S(1)} %copy-done, bf16[8,2,96,2,5,2]{2,1,3,5,4,0:T(2,128)(2,1)S(1)} %bitcast.177), kind=kOutput, calls=%fused_computation.3 | convolution fusion | flops 92765760 | bytes 5505440 | tf_op jit(solution)/shard_map/pqk,kecrph->phercq/dot_general | solution.py:63
  74.4 5.7 %add_convert_fusion = (bf16[5,1,96,1361]{3,2,1,0:T(8,128)(2,1)}, bf16[5,1,96,1361]{3,2,1,0:T(8,128)(2,1)}) fusion(f32[5,2,96,1361]{3,2,1,0:T(8,128)S(1)} %copy-done.6, f32[5,2,96,1361]{3,2,1,0:T(8,128)} %broadcast_select_fusion), kind=kLoop, calls=%fused_computation.28 | loop fusion | flops 5226240 | bytes 13065600 | tf_op jit(solution)/shard_map/convert.2
  80.1 2.6 %multiply_add_fusion = (f32[5,1,96,1361]{3,2,1,0:T(8,128)S(1)}, f32[5,1,96,1361]{3,2,1,0:T(8,128)S(1)}, bf16[5,1,96,1361]{3,2,1,0:T(8,128)(2,1)}, bf16[5,1,96,1361]{3,2,1,0:T(8,128)(2,1)}) fusion(f32[5,2,96,1361]{3,2,1,0:T(8,128)S(1)} %copy-done.6, f32[5,2,96,1361]{3,2,1,0:T(8,128)S(1)} %fusion.1, f32[5,2,96,1361]{3,2,1,0:T(8,128)S(1)} %bitcast.167), kind=kLoop, calls=%fused_computation.26 | loop fusion | flops 9145920 | bytes 23518080 | tf_op jit(solution)/shard_map/add | solution.py:91
  82.7 1.2 fusion.22
  84.6 1.3 broadcast_in_dim.141
  85.9 6.5 %dynamic_update_slice.15 = f32[2,96,2081]{2,1,0:T(8,128)} dynamic-update-slice(f32[2,96,2081]{2,1,0:T(8,128)} %broadcast_in_dim.141, f32[2,96,1361]{2,1,0:T(8,128)} %fusion.22, s32[]{:T(128)} %constant.26.clone.1, s32[]{:T(128)} %constant.26.clone.1, s32[]{:T(128)S(6)} %select_n.118) | dynamic-update-slice | bytes 2090500 | tf_op jit(solution)/shard_map/dynamic_update_slice | solution.py:97
  92.4 2.8 %fusion.26 = f32[2,96,1361]{2,1,0:T(8,128)} fusion(f32[5,1,96,1361]{3,2,1,0:T(8,128)S(1)} %get-tuple-element.17, f32[5,1,96,1361]{3,2,1,0:T(8,128)} %copy-done.1, f32[2,96,2081]{2,1,0:T(8,128)} %dynamic_update_slice.15, s32[]{:T(128)S(6)} %select_n.119, pred[1361]{0:T(1024)(128)(4,1)S(1)} %get-tuple-element.10), kind=kLoop, calls=%fused_computation.59 | loop fusion | flops 783936 | bytes 7318101 | tf_op jit(solution)/shard_map/add | solution.py:97
  95.2 6.5 %dynamic_update_slice.16 = f32[2,96,2081]{2,1,0:T(8,128)} dynamic-update-slice(f32[2,96,2081]{2,1,0:T(8,128)} %dynamic_update_slice.15, f32[2,96,1361]{2,1,0:T(8,128)} %fusion.26, s32[]{:T(128)} %constant.26.clone.1, s32[]{:T(128)} %constant.26.clone.1, s32[]{:T(128)S(6)} %select_n.119) | dynamic-update-slice | bytes 2090500 | tf_op jit(solution)/shard_map/dynamic_update_slice | solution.py:97
  101.7 2.8 %fusion.30 = f32[2,96,1361]{2,1,0:T(8,128)} fusion(f32[5,1,96,1361]{3,2,1,0:T(8,128)S(1)} %get-tuple-element.17, f32[5,1,96,1361]{3,2,1,0:T(8,128)} %copy-done.1, f32[2,96,2081]{2,1,0:T(8,128)} %dynamic_update_slice.16, s32[]{:T(128)S(6)} %select_n.120, pred[1361]{0:T(1024)(128)(4,1)S(1)} %get-tuple-element.9), kind=kLoop, calls=%fused_computation.63 | loop fusion | flops 783936 | bytes 7318101 | tf_op jit(solution)/shard_map/add | solution.py:97
  104.5 6.5 %dynamic_update_slice.17 = f32[2,96,2081]{2,1,0:T(8,128)} dynamic-update-slice(f32[2,96,2081]{2,1,0:T(8,128)} %dynamic_update_slice.16, f32[2,96,1361]{2,1,0:T(8,128)} %fusion.30, s32[]{:T(128)} %constant.26.clone.1, s32[]{:T(128)} %constant.26.clone.1, s32[]{:T(128)S(6)} %select_n.120) | dynamic-update-slice | bytes 2090500 | tf_op jit(solution)/shard_map/dynamic_update_slice | solution.py:97
  110.9 2.2 maximum_convert_fusion
  113.9 9.1 %multiply_convert_fusion = (bf16[5,2,2,2,96,1361]{5,4,1,3,2,0:T(8,128)(2,1)}, bf16[5,2,2,2,96,1361]{5,4,1,3,2,0:T(8,128)(2,1)}) fusion(f32[5,2,96,1361]{3,2,1,0:T(8,128)S(1)} %maximum_convert_fusion.1, f32[5,2,2,1361]{3,1,2,0:T(2,128)S(1)} %and_convert_fusion, f32[5,2,96,1361]{3,2,1,0:T(8,128)S(1)} %maximum_convert_fusion), kind=kLoop, calls=%fused_computation.4 | loop fusion | flops 20904960 | bytes 31466320 | tf_op jit(solution)/shard_map/convert_element_type | solution.py:106
  122.9 6.4 %fusion.2 = f32[5,2,2,2,96,8]{4,5,3,2,1,0:T(8,128)S(1)} fusion(bf16[5,2,2,2,96,1361]{5,4,1,3,2,0:T(8,128)(2,1)} %get-tuple-element.42, bf16[5,1361,8]{1,2,0:T(8,128)(2,1)S(1)} %copy-done), kind=kOutput, calls=%fused_computation.6 | convolution fusion | flops 83619840 | bytes 10684240 | tf_op jit(solution)/shard_map/pqk,phercq->kecrph/dot_general | solution.py:107
  129.4 1.3 fusion.34
  131.4 6.5 %dynamic_update_slice.18 = f32[2,96,2081]{2,1,0:T(8,128)} dynamic-update-slice(f32[2,96,2081]{2,1,0:T(8,128)} %dynamic_update_slice.17, f32[2,96,1361]{2,1,0:T(8,128)} %fusion.34, s32[]{:T(128)} %constant.26.clone.1, s32[]{:T(128)} %constant.26.clone.1, s32[]{:T(128)S(6)} %select_n.121) | dynamic-update-slice | bytes 2090500 | tf_op jit(solution)/shard_map/dynamic_update_slice | solution.py:97
  137.8 1.0 add_convert_fusion.2
  138.8 0.8 pad_maximum_fusion.5
  139.6 4.2 %all-to-all-start.3 = ((bf16[8,2,96,2,10]{2,3,4,1,0:T(2,128)(2,1)}), bf16[8,2,96,2,10]{2,3,4,1,0:T(2,128)(2,1)S(1)}, u32[]{:S(2)}, u32[]{:S(2)}) async-start(bf16[8,2,96,2,10]{2,3,4,1,0:T(2,128)(2,1)} %pad_maximum_fusion.5), calls=%async_computation.3 | async-start | bytes 163840 | tf_op jit(solution)/shard_map/all_to_all | solution.py:114
  143.7 6.4 %fusion.4 = f32[5,2,2,2,96,8]{4,5,3,2,1,0:T(8,128)S(1)} fusion(bf16[5,2,2,2,96,1361]{5,4,1,3,2,0:T(8,128)(2,1)} %get-tuple-element.43, bf16[5,1361,8]{1,2,0:T(8,128)(2,1)S(1)} %copy-done), kind=kOutput, calls=%fused_computation.8 | convolution fusion | flops 83619840 | bytes 10684240 | tf_op jit(solution)/shard_map/pqk,phercq->kecrph/dot_general | solution.py:107
  150.3 1.4 fusion.7
  151.9 1.3 fusion.38
  153.2 0.8 pad_maximum_fusion.3
  154.0 6.5 %dynamic_update_slice.19 = f32[2,96,2081]{2,1,0:T(8,128)} dynamic-update-slice(f32[2,96,2081]{2,1,0:T(8,128)} %dynamic_update_slice.18, f32[2,96,1361]{2,1,0:T(8,128)} %fusion.38, s32[]{:T(128)} %constant.26.clone.1, s32[]{:T(128)} %constant.26.clone.1, s32[]{:T(128)S(6)} %select_n.122) | dynamic-update-slice | bytes 2090500 | tf_op jit(solution)/shard_map/dynamic_update_slice | solution.py:97
  160.5 4.2 %all-to-all-start.1 = ((bf16[8,2,96,2,10]{2,3,4,1,0:T(2,128)(2,1)}), bf16[8,2,96,2,10]{2,3,4,1,0:T(2,128)(2,1)S(1)}, u32[]{:S(2)}, u32[]{:S(2)}) async-start(bf16[8,2,96,2,10]{2,3,4,1,0:T(2,128)(2,1)} %pad_maximum_fusion.3), calls=%async_computation.1 | async-start | bytes 163840 | tf_op jit(solution)/shard_map/all_to_all | solution.py:113
  164.7 2.1 fusion.39
  166.9 2.9 %all-to-all-done.1 = bf16[8,2,96,2,10]{2,3,4,1,0:T(2,128)(2,1)S(1)} async-done(((bf16[8,2,96,2,10]{2,3,4,1,0:T(2,128)(2,1)}), bf16[8,2,96,2,10]{2,3,4,1,0:T(2,128)(2,1)S(1)}, u32[]{:S(2)}, u32[]{:S(2)}) %all-to-all-start.1) | async-done | bytes 61472 | tf_op jit(solution)/shard_map/all_to_all | solution.py:113
  170.0 6.1 %copy.57 = bf16[1,2,384,1440]{2,3,1,0:T(8,128)(2,1)S(1)} copy(bf16[1,2,384,1440]{3,1,0,2:T(2,128)(2,1)} %all-gather.3.cloned.1.call-done) | data formatting | bytes 4423680 | tf_op jit(solution)/shard_map/all_gather | solution.py:124
  176.1 1.2 fusion.17
  177.4 6.9 %copy.69 = bf16[1,2,384,1440]{2,3,1,0:T(8,128)(2,1)} copy(bf16[1,2,384,1440]{3,1,0,2:T(2,128)(2,1)} %all-gather.5.cloned.1.call-done) | data formatting | bytes 4423680 | tf_op jit(solution)/shard_map/all_gather | solution.py:125
  184.3 2.7 %convolution_bitcast_fusion = f32[1,2,96,1440]{3,2,1,0:T(8,128)S(1)} fusion(bf16[1,2,384,1440]{2,3,1,0:T(8,128)(2,1)} %copy.69, bf16[384,384]{0,1:T(8,128)(2,1)} %all_gather.10, s32[]{:T(128)S(6)} %select_n.130), kind=kOutput, calls=%fused_computation.32 | convolution fusion | flops 212336640 | bytes 3416068 | tf_op jit(solution)/shard_map/khoj,io->khij/dot_general | solution.py:132
  187.0 1.2 fusion.11
  188.1 0.8 convolution_bitcast_fusion.2
  188.9 1.2 fusion.10
  190.1 41.2 %all-reduce.5.cloned.1.call-done = (f32[96,2,720]{2,0,1:T(8,128)}, f32[384,96]{0,1:T(8,128)}) async-done(((f32[96,2,720]{2,0,1:T(8,128)}, f32[384,96]{0,1:T(8,128)}), (f32[96,2,720]{2,0,1:T(8,128)}, f32[384,96]{0,1:T(8,128)})) %all-reduce.5.cloned.1.call-update) | async-done | bytes 700432 | tf_op jit(solution)/shard_map/psum | solution.py:140
  231.3 1.1 broadcast_multiply_fusion
  232.5 1.3 copy.70
  233.7 1.6 broadcast_multiply_fusion.1
  (92 shorter events, 7.8 us)
Async XLA Ops:
  7.2 57.5 %copy-start = (bf16[5,1361,8]{1,2,0:T(8,128)(2,1)S(1)}, bf16[5,1361,8]{1,2,0:T(8,128)(2,1)}, u32[]{:S(2)}) copy-start(bf16[5,1361,8]{1,2,0:T(8,128)(2,1)} %param.8) | copy-start | bytes 326644
  7.2 14.7 %copy-start.11 = (bf16[1,2,96,1440]{3,2,1,0:T(8,128)(2,1)S(1)}, bf16[1,2,96,1440]{3,2,1,0:T(8,128)(2,1)}, u32[]{:S(2)}) copy-start(bf16[1,2,96,1440]{3,2,1,0:T(8,128)(2,1)} %param.7) | copy-start | bytes 1658884
  7.2 162.8 %all-gather.3.cloned.1.call-start = ((), (), s32[]{:S(2)}) async-start(), calls=%async_computation.4 | async-start | bytes 2949120 | tf_op jit(solution)/shard_map/all_gather | solution.py:124
  9.8 13.5 %copy-start.19 = (s32[40]{0:T(128)S(1)}, s32[40]{0:T(128)}, u32[]{:S(2)}) copy-start(s32[40]{0:T(128)} %param.11) | copy-start | bytes 484
  9.8 20.7 %copy-start.16 = (bf16[1,2,96,1440]{3,2,1,0:T(8,128)(2,1)S(1)}, bf16[1,2,96,1440]{3,2,1,0:T(8,128)(2,1)}, u32[]{:S(2)}) copy-start(bf16[1,2,96,1440]{3,2,1,0:T(8,128)(2,1)} %param.6) | copy-start | bytes 1658884
  14.2 16.7 %copy-start.12 = (bf16[1440,1,80]{0,2,1:T(8,128)(2,1)}, bf16[1440,1,80]{0,2,1:T(8,128)(2,1)S(1)}, u32[]{:S(2)}) copy-start(bf16[1440,1,80]{0,2,1:T(8,128)(2,1)S(1)} %get-tuple-element.51) | copy-start | bytes 691204
  14.2 16.7 %copy-start.14 = (bf16[1440,1,80]{0,2,1:T(8,128)(2,1)}, bf16[1440,1,80]{0,2,1:T(8,128)(2,1)S(1)}, u32[]{:S(2)}) copy-start(bf16[1440,1,80]{0,2,1:T(8,128)(2,1)S(1)} %get-tuple-element.52) | copy-start | bytes 691204
  14.2 16.7 %copy-start.10 = (f32[96,2,720]{2,1,0:T(2,128)S(1)}, f32[96,2,720]{2,1,0:T(2,128)}, u32[]{:S(2)}) copy-start(f32[96,2,720]{2,1,0:T(2,128)} %param.9) | copy-start | bytes 1658884
  16.6 44.0 %all-to-all-start.2 = ((bf16[1,2,96,2,80]{2,1,3,0,4:T(2,128)(2,1)}), bf16[1,2,96,2,80]{2,1,3,0,4:T(2,128)(2,1)S(1)}, u32[]{:S(2)}, u32[]{:S(2)}) async-start(bf16[1,2,96,2,80]{2,1,3,0,4:T(2,128)(2,1)} %copy.58), calls=%async_computation.2 | async-start | bytes 163840 | tf_op jit(solution)/shard_map/all_to_all | solution.py:42
  21.8 155.6 %all-gather.5.cloned.1.call-start = ((), (), s32[]{:S(2)}) async-start(), calls=%async_computation.5 | async-start | bytes 2949120 | tf_op jit(solution)/shard_map/all_gather | solution.py:125
  38.9 3.1 %copy-start.17 = (bf16[384,96]{0,1:T(8,128)(2,1)S(1)}, bf16[384,96]{0,1:T(8,128)(2,1)}, u32[]{:S(2)}) copy-start(bf16[384,96]{0,1:T(8,128)(2,1)} %param.10) | copy-start | bytes 221188
  60.6 10.1 %all-to-all-start = ((bf16[1,2,96,2,80]{2,1,3,0,4:T(2,128)(2,1)}), bf16[1,2,96,2,80]{2,1,3,0,4:T(2,128)(2,1)S(1)}, u32[]{:S(2)}, u32[]{:S(2)}) async-start(bf16[1,2,96,2,80]{2,1,3,0,4:T(2,128)(2,1)} %copy.47), calls=%async_computation | async-start | bytes 163840 | tf_op jit(solution)/shard_map/all_to_all | solution.py:41
  70.7 3.7 %copy-start.6 = (f32[5,2,96,1361]{3,2,1,0:T(8,128)S(1)}, f32[5,2,96,1361]{3,2,1,0:T(8,128)}, u32[]{:S(2)}) copy-start(f32[5,2,96,1361]{3,2,1,0:T(8,128)} %fusion) | copy-start | bytes 15678724
  70.7 9.4 %slice-start = ((s8[5406720]{0:T(1024)(128)(4,1)}), s8[1212416]{0:T(1024)(128)(4,1)S(1)}, s32[]{:S(2)}) async-start(s8[5406720]{0:T(1024)(128)(4,1)} %bitcast.166), calls=%async_computation.7 | async-start | bytes 2424832
  74.4 5.7 %slice-start.1 = ((s8[5406720]{0:T(1024)(128)(4,1)}), s8[4194304]{0:T(1024)(128)(4,1)S(1)}, s32[]{:S(2)}) async-start(s8[5406720]{0:T(1024)(128)(4,1)} %bitcast.166), calls=%async_computation.8 | async-start | bytes 8388608
  82.7 1.8 copy-start.1
  110.9 2.2 copy-start.7
  110.9 2.5 %copy-start.8 = (bf16[5,1,96,1361]{3,2,1,0:T(8,128)(2,1)S(1)}, bf16[5,1,96,1361]{3,2,1,0:T(8,128)(2,1)}, u32[]{:S(2)}) copy-start(bf16[5,1,96,1361]{3,2,1,0:T(8,128)(2,1)} %get-tuple-element.20) | copy-start | bytes 3919684
  122.9 6.4 %copy-start.2 = (f32[5,1,96,1361]{3,2,1,0:T(8,128)S(1)}, f32[5,1,96,1361]{3,2,1,0:T(8,128)}, u32[]{:S(2)}) copy-start(f32[5,1,96,1361]{3,2,1,0:T(8,128)} %copy-done.1) | copy-start | bytes 7839364
  122.9 6.4 %copy-start.4 = (f32[2,96,2081]{2,1,0:T(8,128)S(1)}, f32[2,96,2081]{2,1,0:T(8,128)}, u32[]{:S(2)}) copy-start(f32[2,96,2081]{2,1,0:T(8,128)} %dynamic_update_slice.17) | copy-start | bytes 4794628
  139.6 20.9 %all-to-all-start.3 = ((bf16[8,2,96,2,10]{2,3,4,1,0:T(2,128)(2,1)}), bf16[8,2,96,2,10]{2,3,4,1,0:T(2,128)(2,1)S(1)}, u32[]{:S(2)}, u32[]{:S(2)}) async-start(bf16[8,2,96,2,10]{2,3,4,1,0:T(2,128)(2,1)} %pad_maximum_fusion.5), calls=%async_computation.3 | async-start | bytes 163840 | tf_op jit(solution)/shard_map/all_to_all | solution.py:114
  143.7 6.6 %copy-start.3 = (f32[5,1,96,1361]{3,2,1,0:T(8,128)S(1)}, f32[5,1,96,1361]{3,2,1,0:T(8,128)}, u32[]{:S(2)}) copy-start(f32[5,1,96,1361]{3,2,1,0:T(8,128)} %copy-done.1) | copy-start | bytes 7839364
  150.3 1.5 copy-start.5
  153.2 11.5 %copy-start.9 = (f32[2,96,1361]{2,1,0:T(8,128)S(1)}, f32[2,96,1361]{2,1,0:T(8,128)}, u32[]{:S(2)}) copy-start(f32[2,96,1361]{2,1,0:T(8,128)} %fusion.7) | copy-start | bytes 3135748
  153.2 16.6 %copy-start.20 = (bf16[80]{0:T(256)(128)(2,1)S(1)}, bf16[80]{0:T(256)(128)(2,1)}, u32[]{:S(2)}) copy-start(bf16[80]{0:T(256)(128)(2,1)} %get-tuple-element.45) | copy-start | bytes 484
  160.5 9.3 %all-to-all-start.1 = ((bf16[8,2,96,2,10]{2,3,4,1,0:T(2,128)(2,1)}), bf16[8,2,96,2,10]{2,3,4,1,0:T(2,128)(2,1)S(1)}, u32[]{:S(2)}, u32[]{:S(2)}) async-start(bf16[8,2,96,2,10]{2,3,4,1,0:T(2,128)(2,1)} %pad_maximum_fusion.3), calls=%async_computation.1 | async-start | bytes 163840 | tf_op jit(solution)/shard_map/all_to_all | solution.py:113
  164.6 66.7 %all-reduce.5.cloned.1.call-start = ((), (), s32[]{:S(2)}) async-start(), calls=%async_computation.6 | async-start | bytes 1474560 | tf_op jit(solution)/shard_map/psum | solution.py:140
  184.3 2.7 %copy-start.13 = (bf16[1440,1,80]{0,2,1:T(8,128)(2,1)S(1)}, bf16[1440,1,80]{0,2,1:T(8,128)(2,1)}, u32[]{:S(2)}) copy-start(bf16[1440,1,80]{0,2,1:T(8,128)(2,1)} %copy-done.12) | copy-start | bytes 691204
  184.3 2.7 %copy-start.15 = (bf16[1440,1,80]{0,2,1:T(8,128)(2,1)S(1)}, bf16[1440,1,80]{0,2,1:T(8,128)(2,1)}, u32[]{:S(2)}) copy-start(bf16[1440,1,80]{0,2,1:T(8,128)(2,1)} %copy-done.14) | copy-start | bytes 691204
  184.3 3.9 %copy-start.18 = (bf16[384,96]{0,1:T(8,128)(2,1)S(1)}, bf16[384,96]{0,1:T(8,128)(2,1)}, u32[]{:S(2)}) copy-start(bf16[384,96]{0,1:T(8,128)(2,1)} %param.10) | copy-start | bytes 221188
Sparse Core Ops, SparseCore 0:
  10.2 57.7 all-gather.2
  70.1 49.2 all-gather.4
  177.5 53.8 all-reduce.4
where the time goes:
time: 244 us; the launch traced here: 242 us
  local copies, waits for them, and re-layouts  60.8 us (25%)
  other arithmetic  45.8 us (19%)
  waiting for transfers between devices  44.2 us (18%)
  matrix products  31.6 us (13%)
  between operations  23.8 us (10%)
  blocking collectives  17.9 us (7%)
  starting transfers between devices  17.7 us (7%)
    psum x1, waiting for transfers between devices, local(): weight_sum, mixing_sum = lax.psum((grad_local, mixing_grad), 'lat')  41.2 us
    dynamic_update_slice x5, local copies, waits for them, and re-layouts, local(): lax.dynamic_update_slice_in_dim(grad_rows, current + head_part, lower[slo...  32.4 us
    all_gather x1, blocking collectives, local(): lax.all_gather(mixing, 'chan', axis=1, tiled=True)  17.9 us
    dot_general x2, matrix products, synthesize(): jnp.einsum('pqk,phercq->kecrph', legendre, masked, preferred_element_type...  12.9 us
    dot_general x2, matrix products, analyse(): jnp.einsum('pqk,kecrph->phercq', legendre, received, preferred_element_ty...  9.7 us
    convert_element_type x1, other arithmetic, synthesize(): masked = (coeff[:, None, None].astype(jnp.float32) * selector[:, :, :, No...  9.06 us
    another operation x6, other arithmetic  9 us
    add x4, other arithmetic, local(): current + head_part  8.28 us
  transfers between devices with their start and end apart: 7, of which 2 were waited for; matrix products, arithmetic and copies ran while one was open for 54% of the time, Pallas kernels for 0%

commit v1 on v0

--- a/solution.py
+++ b/solution.py
@@ -3,6 +3,28 @@
 import jax.numpy as jnp
 from jax import lax
 from jax.sharding import PartitionSpec as P
+
+
+def split_up(x, dim, size):
+    before, after = (x.shape[:dim], x.shape[dim + 1 :])
+    return jnp.moveaxis(x.reshape(*before, size, -1, *after), dim, 0)
+
+
+def in_order(tiles, dim):
+    tiles = jnp.moveaxis(tiles, 0, dim)
+    shape = tiles.shape
+    return tiles.reshape(*shape[:dim], shape[dim] * shape[dim + 1], *shape[dim + 2 :])
+
+
+def pairwise_exchange(x, axis, split_dim, concat_dim):
+    size, here = (lax.axis_size(axis), lax.axis_index(axis))
+    blocks = split_up(x, split_dim, size)
+    outs = [blocks[here]]
+    for lap in range(1, size):
+        sent = blocks[here ^ lap]
+        outs.append(lax.ppermute(sent, axis, [(i, i ^ lap) for i in range(size)]))
+    blocks = jnp.stack(outs)[here ^ jnp.arange(size)]
+    return in_order(blocks, concat_dim)
 
 
 def dft_basis(orders, longitudes):
@@ -39,7 +61,7 @@
     )
     recv_x, recv_g = (
         lax.all_to_all(even_odd(spec_x), "lat", split_axis=4, concat_axis=0, tiled=True),
-        lax.all_to_all(even_odd(spec_g), "lat", split_axis=4, concat_axis=0, tiled=True),
+        pairwise_exchange(even_odd(spec_g), "lat", 4, 0),
     )
     owner_shape = (npairs, 2, chan_width, 2, owned, 2)
     recv_x = recv_x.reshape(owner_shape)

time: 244 us -> 258 us (1.057)
  local copies, waits for them, and re-layouts: 60.8 us -> 73.3 us
  other arithmetic: 45.8 us -> 48.9 us
    unnamed x54 -> x56, local copies, waits for them, and re-layouts: 6.75 us -> 17.8 us
    ppermute x0 -> x7, starting transfers between devices: none -> 7.27 us  [pairwise_exchange(): outs.append(lax.ppermute(sent, axis, [(i, i ^ lap) for i in range(size)]))]
    another operation x6, other arithmetic: 9 us -> 3.5 us
    all_to_all x1 -> x0, starting transfers between devices: 5.17 us -> none  [local(): lax.all_to_all(even_odd(spec_g), 'lat', split_axis=4, concat_axis=0, tile...]
    select_n x1, other arithmetic: 2.78 us -> 5.42 us  [local(): jnp.where(leading[:, None, None, :], picked_lead, weight_tail[None])]
  transfers between devices with their start and end apart: 7 -> 13, of which waited for: 2 -> 3; matrix products, arithmetic and copies ran while one was open for 54% -> 56% of each run, Pallas kernels for 0% -> 0%
where the time goes in v1:
time: 258 us; the launch traced here: 255 us
  local copies, waits for them, and re-layouts  73.3 us (28%)
  other arithmetic  48.9 us (19%)
  waiting for transfers between devices  44.8 us (17%)
  matrix products  29.2 us (11%)
  between operations  24.1 us (9%)
  starting transfers between devices  18.8 us (7%)
  blocking collectives  16.3 us (6%)
    psum x1, waiting for transfers between devices, local(): weight_sum, mixing_sum = lax.psum((grad_local, mixing_grad), 'lat')  40.8 us
    dynamic_update_slice x5, local copies, waits for them, and re-layouts, local(): lax.dynamic_update_slice_in_dim(grad_rows, current + head_part, lower[slo...  32.5 us
    unnamed x56, local copies, waits for them, and re-layouts  17.8 us
    all_gather x1, blocking collectives, local(): lax.all_gather(mixing, 'chan', axis=1, tiled=True)  16.3 us
    dot_general x2, matrix products, synthesize(): jnp.einsum('pqk,phercq->kecrph', legendre, masked, preferred_element_type...  12.9 us
    convert_element_type x1, other arithmetic, synthesize(): masked = (coeff[:, None, None].astype(jnp.float32) * selector[:, :, :, No...  10.7 us
    add x4, other arithmetic, local(): current + head_part  8.23 us
    dot_general x2, matrix products, analyse(): jnp.einsum('pqk,kecrph->phercq', legendre, received, preferred_element_ty...  7.36 us
  transfers between devices with their start and end apart: 13, of which 3 were waited for; matrix products, arithmetic and copies ran while one was open for 56% of the time, Pallas kernels for 0%

profile of v1, /device:TPU:0, one launch (start us, length us, event | category | flops | bytes accessed | tf_op | source)
XLA Modules:
  0.0 255.4 jit_solution(2060392895815714533)
XLA Ops:
  7.2 2.6 copy.77
  11.4 2.3 multiply_convert_fusion.3
  13.8 1.6 fusion.16
  16.6 2.5 collective-permute-start.1
  19.3 1.7 collective-permute-start.3
  22.2 3.9 %all-to-all-start = ((bf16[1,2,96,2,80]{2,1,3,0,4:T(2,128)(2,1)}), bf16[1,2,96,2,80]{2,1,3,0,4:T(2,128)(2,1)S(1)}, u32[]{:S(2)}, u32[]{:S(2)}) async-start(bf16[1,2,96,2,80]{2,1,3,0,4:T(2,128)(2,1)} %copy.68), calls=%async_computation | async-start | bytes 163840 | tf_op jit(solution)/shard_map/all_to_all | solution.py:63
  26.2 1.4 copy.89
  39.1 4.9 %pad_dynamic-slice_fusion = (f32[2,96,1361]{2,0,1:T(2,128)S(1)}, f32[2,96,1361]{2,0,1:T(2,128)}, f32[2,96,1361]{2,0,1:T(2,128)}, f32[2,96,1361]{2,0,1:T(2,128)S(1)}, f32[2,96,1361]{2,0,1:T(2,128)S(1)}) fusion(s32[]{:T(128)S(6)} %select_n.156, f32[2,96,720]{2,0,1:T(2,128)S(1)} %bitcast.203, s32[]{:T(128)S(6)} %select_n.153, s32[]{:T(128)S(6)} %select_n.154, ...), kind=kLoop, calls=%fused_computation.41 | loop fusion | bytes 5779220 | tf_op jit(solution)/shard_map/dynamic_slice | solution.py:100
  45.3 2.4 bitcast_dynamic-update-slice_fusion.3
  47.6 1.1 bitcast_dynamic-update-slice_fusion.2
  51.1 5.4 %broadcast_select_fusion = f32[5,2,96,1361]{3,2,1,0:T(8,128)} fusion(f32[5,2,96,1361]{3,2,1,0:T(8,128)} %bitcast_dynamic-update-slice_fusion, f32[2,96,1361]{2,1,0:T(8,128)S(1)} %concatenate.36.clone, pred[5,1361]{1,0:T(8,128)(4,1)S(1)} %iota_compare_fusion.2), kind=kLoop, calls=%fused_computation.32 | loop fusion | flops 1306560 | bytes 11504533 | tf_op jit(solution)/shard_map/jit(_where)/select_n | solution.py:102
  56.8 16.3 %all_gather.10 = bf16[384,384]{0,1:T(8,128)(2,1)} all-gather(bf16[384,96]{0,1:T(8,128)(2,1)S(1)} %copy-done.17), channel_id=1, replica_groups=mesh['lat'=8,'chan'=4] {'chan'}, dimensions={1}, use_global_device_ids=true | all-gather | bytes 368640 | tf_op jit(solution)/shard_map/all_gather | solution.py:148
  73.1 2.4 collective-permute-start.5
  81.0 3.7 %fusion = f32[5,2,96,1361]{3,2,1,0:T(8,128)S(1)} fusion(f32[5,2,2,1361]{3,1,2,0:T(2,128)S(1)} %and_convert_fusion, bf16[5,1361,8]{1,2,0:T(8,128)(2,1)S(1)} %copy-done, bf16[8,2,96,2,5,2]{2,3,5,4,1,0:T(2,128)(2,1)S(1)} %bitcast.201), kind=kOutput, calls=%fused_computation.2 | convolution fusion | flops 92765760 | bytes 5505440 | tf_op jit(solution)/shard_map/pqk,kecrph->phercq/dot_general | solution.py:85
  85.8 1.4 copy-done.6
  87.2 2.8 %maximum_convert_fusion.1 = f32[5,2,96,1361]{3,2,1,0:T(8,128)} fusion(bf16[5,1,96,1361]{3,2,1,0:T(8,128)(2,1)S(1)} %get-tuple-element.20, bf16[5,1,96,1361]{3,2,1,0:T(8,128)(2,1)S(1)} %get-tuple-element.19), kind=kLoop, calls=%fused_computation.25 | loop fusion | flops 2613120 | bytes 7839360 | tf_op jit(solution)/shard_map/convert_element_type | solution.py:127
  90.0 3.7 %fusion.1 = f32[5,2,96,1361]{3,2,1,0:T(8,128)S(1)} fusion(f32[5,2,2,1361]{3,1,2,0:T(2,128)S(1)} %and_convert_fusion, bf16[5,1361,8]{1,2,0:T(8,128)(2,1)S(1)} %copy-done, bf16[8,2,96,2,5,2]{2,1,3,5,4,0:T(2,128)(2,1)S(1)} %bitcast.214), kind=kOutput, calls=%fused_computation.4 | convolution fusion | flops 92765760 | bytes 5505440 | tf_op jit(solution)/shard_map/pqk,kecrph->phercq/dot_general | solution.py:85
  93.7 4.5 %multiply_add_fusion = (f32[5,1,96,1361]{3,2,1,0:T(8,128)S(1)}, f32[5,1,96,1361]{3,2,1,0:T(8,128)S(1)}, bf16[5,1,96,1361]{3,2,1,0:T(8,128)(2,1)}, bf16[5,1,96,1361]{3,2,1,0:T(8,128)(2,1)}) fusion(f32[5,2,96,1361]{3,2,1,0:T(8,128)S(1)} %copy-done.7, f32[5,2,96,1361]{3,2,1,0:T(8,128)S(1)} %fusion.1, f32[5,2,96,1361]{3,2,1,0:T(8,128)} %broadcast_select_fusion), kind=kLoop, calls=%fused_computation.27 | loop fusion | flops 9145920 | bytes 23518080 | tf_op jit(solution)/shard_map/add | solution.py:113
  98.2 1.1 fusion.22
  100.2 1.3 broadcast_in_dim.142
  101.4 6.5 %dynamic_update_slice.15 = f32[2,96,2081]{2,1,0:T(8,128)} dynamic-update-slice(f32[2,96,2081]{2,1,0:T(8,128)} %broadcast_in_dim.142, f32[2,96,1361]{2,1,0:T(8,128)} %fusion.22, s32[]{:T(128)} %constant.31.clone.1, s32[]{:T(128)} %constant.31.clone.1, s32[]{:T(128)S(6)} %select_n.152) | dynamic-update-slice | bytes 2090500 | tf_op jit(solution)/shard_map/dynamic_update_slice | solution.py:119
  107.9 2.8 %fusion.26 = f32[2,96,1361]{2,1,0:T(8,128)} fusion(f32[5,1,96,1361]{3,2,1,0:T(8,128)S(1)} %get-tuple-element.17, f32[5,1,96,1361]{3,2,1,0:T(8,128)} %copy-done.1, f32[2,96,2081]{2,1,0:T(8,128)} %dynamic_update_slice.15, s32[]{:T(128)S(6)} %select_n.153, pred[1361]{0:T(1024)(128)(4,1)S(1)} %get-tuple-element.10), kind=kLoop, calls=%fused_computation.60 | loop fusion | flops 783936 | bytes 7318101 | tf_op jit(solution)/shard_map/add | solution.py:119
  110.7 6.5 %dynamic_update_slice.16 = f32[2,96,2081]{2,1,0:T(8,128)} dynamic-update-slice(f32[2,96,2081]{2,1,0:T(8,128)} %dynamic_update_slice.15, f32[2,96,1361]{2,1,0:T(8,128)} %fusion.26, s32[]{:T(128)} %constant.31.clone.1, s32[]{:T(128)} %constant.31.clone.1, s32[]{:T(128)S(6)} %select_n.153) | dynamic-update-slice | bytes 2090500 | tf_op jit(solution)/shard_map/dynamic_update_slice | solution.py:119
  117.2 2.8 %fusion.30 = f32[2,96,1361]{2,1,0:T(8,128)} fusion(f32[5,1,96,1361]{3,2,1,0:T(8,128)S(1)} %get-tuple-element.17, f32[5,1,96,1361]{3,2,1,0:T(8,128)} %copy-done.1, f32[2,96,2081]{2,1,0:T(8,128)} %dynamic_update_slice.16, s32[]{:T(128)S(6)} %select_n.154, pred[1361]{0:T(1024)(128)(4,1)S(1)} %get-tuple-element.9), kind=kLoop, calls=%fused_computation.64 | loop fusion | flops 783936 | bytes 7318101 | tf_op jit(solution)/shard_map/add | solution.py:119
  120.0 6.5 %dynamic_update_slice.17 = f32[2,96,2081]{2,1,0:T(8,128)} dynamic-update-slice(f32[2,96,2081]{2,1,0:T(8,128)} %dynamic_update_slice.16, f32[2,96,1361]{2,1,0:T(8,128)} %fusion.30, s32[]{:T(128)} %constant.31.clone.1, s32[]{:T(128)} %constant.31.clone.1, s32[]{:T(128)S(6)} %select_n.154) | dynamic-update-slice | bytes 2090500 | tf_op jit(solution)/shard_map/dynamic_update_slice | solution.py:119
  126.5 2.1 maximum_convert_fusion
  128.6 10.7 %multiply_convert_fusion = (bf16[5,2,2,2,96,1361]{5,4,1,3,2,0:T(8,128)(2,1)}, bf16[5,2,2,2,96,1361]{5,4,1,3,2,0:T(8,128)(2,1)}) fusion(f32[5,2,96,1361]{3,2,1,0:T(8,128)} %maximum_convert_fusion.1, f32[5,2,2,1361]{3,1,2,0:T(2,128)S(1)} %and_convert_fusion, f32[5,2,96,1361]{3,2,1,0:T(8,128)S(1)} %maximum_convert_fusion), kind=kLoop, calls=%fused_computation.5 | loop fusion | flops 20904960 | bytes 31466320 | tf_op jit(solution)/shard_map/convert_element_type | solution.py:128
  139.3 6.4 %fusion.2 = f32[5,2,2,2,96,8]{4,5,3,2,1,0:T(8,128)S(1)} fusion(bf16[5,2,2,2,96,1361]{5,4,1,3,2,0:T(8,128)(2,1)} %get-tuple-element.49, bf16[5,1361,8]{1,2,0:T(8,128)(2,1)S(1)} %copy-done), kind=kOutput, calls=%fused_computation.7 | convolution fusion | flops 83619840 | bytes 10684240 | tf_op jit(solution)/shard_map/pqk,phercq->kecrph/dot_general | solution.py:129
  145.7 1.3 fusion.34
  147.1 6.5 %dynamic_update_slice.18 = f32[2,96,2081]{2,1,0:T(8,128)} dynamic-update-slice(f32[2,96,2081]{2,1,0:T(8,128)} %dynamic_update_slice.17, f32[2,96,1361]{2,1,0:T(8,128)} %fusion.34, s32[]{:T(128)} %constant.31.clone.1, s32[]{:T(128)} %constant.31.clone.1, s32[]{:T(128)S(6)} %select_n.155) | dynamic-update-slice | bytes 2090500 | tf_op jit(solution)/shard_map/dynamic_update_slice | solution.py:119
  154.5 3.6 %all-to-all-start.2 = ((bf16[8,2,96,2,10]{2,3,4,1,0:T(2,128)(2,1)}), bf16[8,2,96,2,10]{2,3,4,1,0:T(2,128)(2,1)S(1)}, u32[]{:S(2)}, u32[]{:S(2)}) async-start(bf16[8,2,96,2,10]{2,3,4,1,0:T(2,128)(2,1)} %pad_maximum_fusion.4), calls=%async_computation.2 | async-start | bytes 163840 | tf_op jit(solution)/shard_map/all_to_all | solution.py:136
  158.1 6.4 %fusion.4 = f32[5,2,2,2,96,8]{4,5,3,2,1,0:T(8,128)S(1)} fusion(bf16[5,2,2,2,96,1361]{5,4,1,3,2,0:T(8,128)(2,1)} %get-tuple-element.50, bf16[5,1361,8]{1,2,0:T(8,128)(2,1)S(1)} %copy-done), kind=kOutput, calls=%fused_computation.9 | convolution fusion | flops 83619840 | bytes 10684240 | tf_op jit(solution)/shard_map/pqk,phercq->kecrph/dot_general | solution.py:129
  164.7 1.4 fusion.7
  166.2 1.3 fusion.38
  168.3 6.5 %dynamic_update_slice.19 = f32[2,96,2081]{2,1,0:T(8,128)} dynamic-update-slice(f32[2,96,2081]{2,1,0:T(8,128)} %dynamic_update_slice.18, f32[2,96,1361]{2,1,0:T(8,128)} %fusion.38, s32[]{:T(128)} %constant.31.clone.1, s32[]{:T(128)} %constant.31.clone.1, s32[]{:T(128)S(6)} %select_n.156) | dynamic-update-slice | bytes 2090500 | tf_op jit(solution)/shard_map/dynamic_update_slice | solution.py:119
  174.8 3.9 %all-to-all-start.1 = ((bf16[8,2,96,2,10]{2,3,4,1,0:T(2,128)(2,1)}), bf16[8,2,96,2,10]{2,3,4,1,0:T(2,128)(2,1)S(1)}, u32[]{:S(2)}, u32[]{:S(2)}) async-start(bf16[8,2,96,2,10]{2,3,4,1,0:T(2,128)(2,1)} %pad_maximum_fusion.3), calls=%async_computation.1 | async-start | bytes 163840 | tf_op jit(solution)/shard_map/all_to_all | solution.py:135
  178.7 2.1 fusion.39
  180.9 2.9 %all-to-all-done.1 = bf16[8,2,96,2,10]{2,3,4,1,0:T(2,128)(2,1)S(1)} async-done(((bf16[8,2,96,2,10]{2,3,4,1,0:T(2,128)(2,1)}), bf16[8,2,96,2,10]{2,3,4,1,0:T(2,128)(2,1)S(1)}, u32[]{:S(2)}, u32[]{:S(2)}) %all-to-all-start.1) | async-done | bytes 61472 | tf_op jit(solution)/shard_map/all_to_all | solution.py:135
  184.1 6.1 %copy.78 = bf16[1,2,384,1440]{2,3,1,0:T(8,128)(2,1)S(1)} copy(bf16[1,2,384,1440]{3,1,0,2:T(2,128)(2,1)} %all-gather.3.cloned.1.call-done) | data formatting | bytes 4423680 | tf_op jit(solution)/shard_map/all_gather | solution.py:146
  190.2 1.2 fusion.17
  191.4 6.8 %copy.90 = bf16[1,2,384,1440]{2,3,1,0:T(8,128)(2,1)} copy(bf16[1,2,384,1440]{3,1,0,2:T(2,128)(2,1)} %all-gather.5.cloned.1.call-done) | data formatting | bytes 4423680 | tf_op jit(solution)/shard_map/all_gather | solution.py:147
  198.3 2.7 %convolution_bitcast_fusion = f32[1,2,96,1440]{3,2,1,0:T(8,128)S(1)} fusion(bf16[1,2,384,1440]{2,3,1,0:T(8,128)(2,1)} %copy.90, bf16[384,384]{0,1:T(8,128)(2,1)} %all_gather.10, s32[]{:T(128)S(6)} %select_n.173), kind=kOutput, calls=%fused_computation.33 | convolution fusion | flops 212336640 | bytes 3416068 | tf_op jit(solution)/shard_map/khoj,io->khij/dot_general | solution.py:154
  201.0 1.2 fusion.11
  202.9 1.2 fusion.10
  204.1 40.8 %all-reduce.5.cloned.1.call-done = (f32[96,2,720]{2,0,1:T(8,128)}, f32[384,96]{0,1:T(8,128)}) async-done(((f32[96,2,720]{2,0,1:T(8,128)}, f32[384,96]{0,1:T(8,128)}), (f32[96,2,720]{2,0,1:T(8,128)}, f32[384,96]{0,1:T(8,128)})) %all-reduce.5.cloned.1.call-update) | async-done | bytes 700432 | tf_op jit(solution)/shard_map/psum | solution.py:162
  244.9 1.1 broadcast_multiply_fusion
  246.0 1.3 copy.91
  247.2 1.6 broadcast_multiply_fusion.1
  (112 shorter events, 20.1 us)
Async XLA Ops:
  7.2 73.8 %copy-start = (bf16[5,1361,8]{1,2,0:T(8,128)(2,1)S(1)}, bf16[5,1361,8]{1,2,0:T(8,128)(2,1)}, u32[]{:S(2)}) copy-start(bf16[5,1361,8]{1,2,0:T(8,128)(2,1)} %param.8) | copy-start | bytes 326644
  7.2 13.8 %copy-start.16 = (bf16[1,2,96,1440]{3,2,1,0:T(8,128)(2,1)S(1)}, bf16[1,2,96,1440]{3,2,1,0:T(8,128)(2,1)}, u32[]{:S(2)}) copy-start(bf16[1,2,96,1440]{3,2,1,0:T(8,128)(2,1)} %param.6) | copy-start | bytes 1658884
  7.2 176.9 %all-gather.3.cloned.1.call-start = ((), (), s32[]{:S(2)}) async-start(), calls=%async_computation.3 | async-start | bytes 2949120 | tf_op jit(solution)/shard_map/all_gather | solution.py:146
  9.8 16.4 %copy-start.12 = (bf16[1,2,96,1440]{3,2,1,0:T(8,128)(2,1)S(1)}, bf16[1,2,96,1440]{3,2,1,0:T(8,128)(2,1)}, u32[]{:S(2)}) copy-start(bf16[1,2,96,1440]{3,2,1,0:T(8,128)(2,1)} %param.7) | copy-start | bytes 1658884
  13.7 13.9 %copy-start.14 = (bf16[1440,1,80]{0,2,1:T(8,128)(2,1)}, bf16[1440,1,80]{0,2,1:T(8,128)(2,1)S(1)}, u32[]{:S(2)}) copy-start(bf16[1440,1,80]{0,2,1:T(8,128)(2,1)S(1)} %get-tuple-element.59) | copy-start | bytes 691204
  13.7 13.9 %copy-start.18 = (s32[40]{0:T(128)S(1)}, s32[40]{0:T(128)}, u32[]{:S(2)}) copy-start(s32[40]{0:T(128)} %param.11) | copy-start | bytes 484
  13.7 21.2 %copy-start.10 = (f32[96,2,720]{2,1,0:T(2,128)S(1)}, f32[96,2,720]{2,1,0:T(2,128)}, u32[]{:S(2)}) copy-start(f32[96,2,720]{2,1,0:T(2,128)} %param.9) | copy-start | bytes 1658884
  16.2 56.9 %collective-permute-start = (bf16[1,2,96,2,10]{2,3,4,1,0:T(2,128)(2,1)}, bf16[1,2,96,2,10]{2,3,4,1,0:T(2,128)(2,1)}, u32[]{:S(2)}, u32[]{:S(2)}) collective-permute-start(bf16[1,2,96,2,10]{2,3,4,1,0:T(2,128)(2,1)} %get-tuple-element.40), channel_id=1, source_target_pairs={{0,4},{4,0},{8,12},{12,8},{16,20},{20,16},{24,28},{28,24},{1,5},{5... | collective-permute-start | bytes 23048 | tf_op jit(solution)/shard_map/ppermute | solution.py:25
  16.6 59.5 %collective-permute-start.1 = (bf16[1,2,96,2,10]{2,3,4,1,0:T(2,128)(2,1)}, bf16[1,2,96,2,10]{2,3,4,1,0:T(2,128)(2,1)}, u32[]{:S(2)}, u32[]{:S(2)}) collective-permute-start(bf16[1,2,96,2,10]{2,3,4,1,0:T(2,128)(2,1)} %get-tuple-element.39), channel_id=1, source_target_pairs={{0,8},{4,12},{8,0},{12,4},{16,24},{20,28},{24,16},{28,20},{1,9},{5... | collective-permute-start | bytes 23048 | tf_op jit(solution)/shard_map/ppermute | solution.py:25
  19.1 57.9 %collective-permute-start.2 = (bf16[1,2,96,2,10]{2,3,4,1,0:T(2,128)(2,1)S(1)}, bf16[1,2,96,2,10]{2,3,4,1,0:T(2,128)(2,1)}, u32[]{:S(2)}, u32[]{:S(2)}) collective-permute-start(bf16[1,2,96,2,10]{2,3,4,1,0:T(2,128)(2,1)S(1)} %get-tuple-element.38), channel_id=1, source_target_pairs={{0,12},{4,8},{8,4},{12,0},{16,28},{20,24},{24,20},{28,16},{1,13},{... | collective-permute-start | bytes 23048 | tf_op jit(solution)/shard_map/ppermute | solution.py:25
  19.3 58.4 %collective-permute-start.3 = (bf16[1,2,96,2,10]{2,3,4,1,0:T(2,128)(2,1)S(1)}, bf16[1,2,96,2,10]{2,3,4,1,0:T(2,128)(2,1)}, u32[]{:S(2)}, u32[]{:S(2)}) collective-permute-start(bf16[1,2,96,2,10]{2,3,4,1,0:T(2,128)(2,1)S(1)} %get-tuple-element.37), channel_id=1, source_target_pairs={{0,16},{4,20},{8,24},{12,28},{16,0},{20,4},{24,8},{28,12},{1,17},{... | collective-permute-start | bytes 23048 | tf_op jit(solution)/shard_map/ppermute | solution.py:25
  21.0 57.4 %collective-permute-start.4 = (bf16[1,2,96,2,10]{2,3,4,1,0:T(2,128)(2,1)S(1)}, bf16[1,2,96,2,10]{2,3,4,1,0:T(2,128)(2,1)}, u32[]{:S(2)}, u32[]{:S(2)}) collective-permute-start(bf16[1,2,96,2,10]{2,3,4,1,0:T(2,128)(2,1)S(1)} %get-tuple-element.36), channel_id=1, source_target_pairs={{0,20},{4,16},{8,28},{12,24},{16,4},{20,0},{24,12},{28,8},{1,21},{... | collective-permute-start | bytes 23048 | tf_op jit(solution)/shard_map/ppermute | solution.py:25
  22.2 67.8 %all-to-all-start = ((bf16[1,2,96,2,80]{2,1,3,0,4:T(2,128)(2,1)}), bf16[1,2,96,2,80]{2,1,3,0,4:T(2,128)(2,1)S(1)}, u32[]{:S(2)}, u32[]{:S(2)}) async-start(bf16[1,2,96,2,80]{2,1,3,0,4:T(2,128)(2,1)} %copy.68), calls=%async_computation | async-start | bytes 163840 | tf_op jit(solution)/shard_map/all_to_all | solution.py:63
  26.1 165.3 %all-gather.5.cloned.1.call-start = ((), (), s32[]{:S(2)}) async-start(), calls=%async_computation.4 | async-start | bytes 2949120 | tf_op jit(solution)/shard_map/all_gather | solution.py:147
  45.1 2.5 copy-start.8
  48.8 2.1 copy-start.11
  51.1 5.7 %copy-start.17 = (bf16[384,96]{0,1:T(8,128)(2,1)S(1)}, bf16[384,96]{0,1:T(8,128)(2,1)}, u32[]{:S(2)}) copy-start(bf16[384,96]{0,1:T(8,128)(2,1)} %param.10) | copy-start | bytes 221188
  73.1 6.1 %collective-permute-start.5 = (bf16[1,2,96,2,10]{2,3,4,1,0:T(2,128)(2,1)S(1)}, bf16[1,2,96,2,10]{2,3,4,1,0:T(2,128)(2,1)S(1)}, u32[]{:S(2)}, u32[]{:S(2)}) collective-permute-start(bf16[1,2,96,2,10]{2,3,4,1,0:T(2,128)(2,1)S(1)} %get-tuple-element.35), channel_id=1, source_target_pairs={{0,24},{4,28},{8,16},{12,20},{16,8},{20,12},{24,0},{28,4},{1,25},{... | collective-permute-start | bytes 23048 | tf_op jit(solution)/shard_map/ppermute | solution.py:25
  76.2 4.1 %collective-permute-start.6 = (bf16[1,2,96,2,10]{2,3,4,1,0:T(2,128)(2,1)S(1)}, bf16[1,2,96,2,10]{2,3,4,1,0:T(2,128)(2,1)S(1)}, u32[]{:S(2)}, u32[]{:S(2)}) collective-permute-start(bf16[1,2,96,2,10]{2,3,4,1,0:T(2,128)(2,1)S(1)} %get-tuple-element.34), channel_id=1, source_target_pairs={{0,28},{4,24},{8,20},{12,16},{16,12},{20,8},{24,4},{28,0},{1,29},{... | collective-permute-start | bytes 23048 | tf_op jit(solution)/shard_map/ppermute | solution.py:25
  80.3 4.4 %slice-start = ((s8[5406720]{0:T(1024)(128)(4,1)}), s8[1212416]{0:T(1024)(128)(4,1)S(1)}, s32[]{:S(2)}) async-start(s8[5406720]{0:T(1024)(128)(4,1)} %bitcast.198), calls=%async_computation.6 | async-start | bytes 2424832
  81.0 3.7 %slice-start.1 = ((s8[5406720]{0:T(1024)(128)(4,1)}), s8[4194304]{0:T(1024)(128)(4,1)S(1)}, s32[]{:S(2)}) async-start(s8[5406720]{0:T(1024)(128)(4,1)} %bitcast.198), calls=%async_computation.7 | async-start | bytes 8388608
  84.7 2.5 copy-start.6
  90.0 3.7 %copy-start.7 = (f32[5,2,96,1361]{3,2,1,0:T(8,128)S(1)}, f32[5,2,96,1361]{3,2,1,0:T(8,128)}, u32[]{:S(2)}) copy-start(f32[5,2,96,1361]{3,2,1,0:T(8,128)} %copy-done.6) | copy-start | bytes 15678724
  98.2 2.0 copy-start.1
  139.3 6.4 %copy-start.2 = (f32[5,1,96,1361]{3,2,1,0:T(8,128)S(1)}, f32[5,1,96,1361]{3,2,1,0:T(8,128)}, u32[]{:S(2)}) copy-start(f32[5,1,96,1361]{3,2,1,0:T(8,128)} %copy-done.1) | copy-start | bytes 7839364
  139.3 6.4 %copy-start.4 = (f32[2,96,2081]{2,1,0:T(8,128)S(1)}, f32[2,96,2081]{2,1,0:T(8,128)}, u32[]{:S(2)}) copy-start(f32[2,96,2081]{2,1,0:T(8,128)} %dynamic_update_slice.17) | copy-start | bytes 4794628
  154.5 20.3 %all-to-all-start.2 = ((bf16[8,2,96,2,10]{2,3,4,1,0:T(2,128)(2,1)}), bf16[8,2,96,2,10]{2,3,4,1,0:T(2,128)(2,1)S(1)}, u32[]{:S(2)}, u32[]{:S(2)}) async-start(bf16[8,2,96,2,10]{2,3,4,1,0:T(2,128)(2,1)} %pad_maximum_fusion.4), calls=%async_computation.2 | async-start | bytes 163840 | tf_op jit(solution)/shard_map/all_to_all | solution.py:136
  158.1 6.6 %copy-start.3 = (f32[5,1,96,1361]{3,2,1,0:T(8,128)S(1)}, f32[5,1,96,1361]{3,2,1,0:T(8,128)}, u32[]{:S(2)}) copy-start(f32[5,1,96,1361]{3,2,1,0:T(8,128)} %copy-done.1) | copy-start | bytes 7839364
  164.6 1.5 copy-start.5
  167.5 11.2 %copy-start.9 = (f32[2,96,1361]{2,1,0:T(8,128)S(1)}, f32[2,96,1361]{2,1,0:T(8,128)}, u32[]{:S(2)}) copy-start(f32[2,96,1361]{2,1,0:T(8,128)} %fusion.7) | copy-start | bytes 3135748
  174.8 9.0 %all-to-all-start.1 = ((bf16[8,2,96,2,10]{2,3,4,1,0:T(2,128)(2,1)}), bf16[8,2,96,2,10]{2,3,4,1,0:T(2,128)(2,1)S(1)}, u32[]{:S(2)}, u32[]{:S(2)}) async-start(bf16[8,2,96,2,10]{2,3,4,1,0:T(2,128)(2,1)} %pad_maximum_fusion.3), calls=%async_computation.1 | async-start | bytes 163840 | tf_op jit(solution)/shard_map/all_to_all | solution.py:135
  178.7 66.2 %all-reduce.5.cloned.1.call-start = ((), (), s32[]{:S(2)}) async-start(), calls=%async_computation.5 | async-start | bytes 1474560 | tf_op jit(solution)/shard_map/psum | solution.py:162
  180.9 9.3 %copy-start.13 = (bf16[1,2,96,1440]{3,2,1,0:T(8,128)(2,1)S(1)}, bf16[1,2,96,1440]{3,2,1,0:T(8,128)(2,1)}, u32[]{:S(2)}) copy-start(bf16[1,2,96,1440]{3,2,1,0:T(8,128)(2,1)} %param.7) | copy-start | bytes 1658884
  198.3 2.7 %copy-start.15 = (bf16[1440,1,80]{0,2,1:T(8,128)(2,1)S(1)}, bf16[1440,1,80]{0,2,1:T(8,128)(2,1)}, u32[]{:S(2)}) copy-start(bf16[1440,1,80]{0,2,1:T(8,128)(2,1)} %copy-done.14) | copy-start | bytes 691204
Sparse Core Ops, SparseCore 0:
  10.2 53.8 all-gather.2
  66.2 49.4 all-gather.4
  191.5 53.2 all-reduce.4
